TPU v7x, 512 devices: a whole 4x8x8 slice. The times are simulated.
512 devices in a mesh: sub: 64 (over x, y, core), grp: 8 (over z).
Axes of the slice: x: 4, y: 8, z: 8, core: 2. Of those that a mesh axis runs over, the one named last changes fastest.
Arguments:
- schur: bfloat16 [64, 8, 1536, 1536], P('sub', 'grp'), as said below
- dual_load: float32 [64, 8, 16, 1536], P('sub', 'grp'), may hold values from -6 to 6
- modes: float32 [64, 8, 6, 1536], P('sub', 'grp'), may hold values from -0.15625 to 0.15625
- diag_stiff: float32 [64, 8, 1536], P('sub', 'grp'), may hold values from 0.5 to 4
- coarse_inverse: float32 [3072, 3072], P(('sub', 'grp')), as said below
- rigid_loads: float32 [64, 8, 6, 16], P('sub', 'grp'), may hold values from -24 to 24
- face_index: int32 [64, 8, 1536], P('sub', 'grp'), may hold values from 0 to 1535, each once within a row
Outputs:
- multipliers: float32 [64, 8, 16, 1536], P('sub', 'grp')
- projected_residual: float32 [64, 8, 16, 1536], P('sub', 'grp')
- amplitudes: float32 [64, 8, 6, 16], P('sub', 'grp')
Inputs may be any that keep to these rules, and one draw needn't show every extreme that they name: Each subdomain's schur is symmetric positive definite. coarse_inverse is symmetric positive definite. Each subdomain's face_index is a permutation of its 1536 dofs.
All inputs are finite; a program needn't handle non-finite values.
Results may differ from a plain program's by a relative error of at most 0.0034.
Values sent between devices are 32-bit elements; how exact they have to be, the bound alone decides.
A program may use at most 64 MiB of HBM per device.

v0:
```python
import jax
import jax.numpy as jnp
from jax import lax
from jax.sharding import PartitionSpec as P


def extended_2(array, sides, width):
    for axis, dim in sides:
        count, length = (lax.axis_size(axis), array.shape[dim])
        up = [(i, (i + 1) % count) for i in range(count - 1)]
        down = [(j, i) for i, j in up]
        last = lax.slice_in_dim(array, length - width, length, axis=dim)
        initial = lax.slice_in_dim(array, 0, width, axis=dim)
        before = lax.ppermute(last, axis, up)
        after = lax.ppermute(initial, axis, down)
        array = jnp.concatenate([before, array, after], axis=dim)
    return array


def neighbours(values):
    rows = values.shape[0]
    width = values.shape[1] // 6
    faces = values.reshape(rows, 6, width)
    lower_row = jnp.stack(
        [
            jnp.concatenate([faces[:, 0], faces[:, 2]], axis=1),
            jnp.concatenate([faces[:, 0], faces[:, 3]], axis=1),
        ],
        axis=0,
    )
    upper_row = jnp.stack(
        [
            jnp.concatenate([faces[:, 1], faces[:, 2]], axis=1),
            jnp.concatenate([faces[:, 1], faces[:, 3]], axis=1),
        ],
        axis=0,
    )
    packed = jnp.stack([lower_row, upper_row], axis=0)
    extended = extended_2(packed, (("sub", 0), ("grp", 1)), 1)
    from_lower_sub = extended[0, 1, :, :width]
    from_upper_sub = extended[3, 1, :, :width]
    from_lower_grp = extended[1, 0, :, width:]
    from_upper_grp = extended[1, 3, :, width:]
    empty = jnp.zeros_like(faces[:, 0])
    joined = jnp.stack(
        [from_lower_sub, from_upper_sub, from_lower_grp, from_upper_grp, empty, empty], axis=1
    )
    return joined.reshape(values.shape)


def assemble(values):
    return values - neighbours(values)


def body(schur, dual_load, modes, diag_stiff, coarse_inverse, rigid_loads, face_index):
    ordering = face_index[0, 0]
    restore = jnp.argsort(ordering)
    schur_face = jnp.take(jnp.take(schur[0, 0], ordering, axis=0), ordering, axis=1)
    load = jnp.take(dual_load[0, 0], ordering, axis=1)
    rigid_modes = jnp.take(modes[0, 0], ordering, axis=1)
    stiffness = jnp.take(diag_stiff[0, 0], ordering, axis=0)
    cases = load.shape[0]
    face_width = ordering.shape[0] // 6
    sub_pos = lax.axis_index("sub")
    grp_pos = lax.axis_index("grp")
    flags = jnp.stack(
        [
            sub_pos > 0,
            sub_pos < lax.axis_size("sub") - 1,
            grp_pos > 0,
            grp_pos < lax.axis_size("grp") - 1,
            sub_pos < 0,
            sub_pos < 0,
        ]
    )
    weights = jnp.repeat(jnp.where(flags, 0.5, 1.0).astype(jnp.float32), face_width)

    def coarse(local_sums):
        gathered = lax.all_gather(local_sums, ("sub", "grp"), axis=0, tiled=True)
        return jnp.dot(
            coarse_inverse,
            gathered,
            precision=lax.Precision.HIGHEST,
            preferred_element_type=jnp.float32,
        )

    def lift(amplitudes):
        return jnp.dot(
            amplitudes.T,
            rigid_modes,
            precision=lax.Precision.HIGHEST,
            preferred_element_type=jnp.float32,
        )

    def project(values):
        local_sums = jnp.dot(
            rigid_modes,
            values.T,
            precision=lax.Precision.HIGHEST,
            preferred_element_type=jnp.float32,
        )
        amplitudes = coarse(local_sums)
        return (values - assemble(lift(amplitudes)), amplitudes)

    def apply_schur(values):
        return jnp.dot(values.astype(jnp.bfloat16), schur_face, preferred_element_type=jnp.float32)

    lifted = lift(coarse(rigid_loads[0, 0]))
    stacked = jnp.concatenate([lifted, stiffness[None, :]], axis=0)
    beside_all = neighbours(stacked)
    multipliers = lifted - beside_all[:cases]
    scaling = stiffness + beside_all[cases]
    residual = assemble(load - apply_schur(multipliers))
    projected, amplitudes = project(residual)
    norm_now = lax.psum(jnp.sum(weights * scaling * projected * projected, axis=1), ("sub", "grp"))
    direction, unused = project(scaling * projected)
    image_local = apply_schur(direction)
    image = assemble(image_local)
    terms = jnp.sum(weights * direction * image, axis=1)
    curvature = lax.psum(terms, ("sub", "grp"))
    step_size = (norm_now / curvature)[:, None]
    multipliers = multipliers + step_size * direction
    residual = residual - step_size * image
    projected, amplitudes = project(residual)
    return (
        jnp.take(multipliers, restore, axis=1)[None, None],
        jnp.take(projected, restore, axis=1)[None, None],
        amplitudes[None, None],
    )


def solution(mesh):
    placed = (
        P("sub", "grp", None, None),
        P("sub", "grp", None, None),
        P("sub", "grp", None, None),
        P("sub", "grp", None),
        P(("sub", "grp"), None),
        P("sub", "grp", None, None),
        P("sub", "grp", None),
    )
    return jax.shard_map(
        body,
        mesh=mesh,
        in_specs=placed,
        out_specs=(
            P("sub", "grp", None, None),
            P("sub", "grp", None, None),
            P("sub", "grp", None, None),
        ),
        check_vma=False,
    )
```

profile of v0, /device:TPU:1, one launch (start us, length us, event | category | flops | bytes accessed | tf_op | source)
XLA Modules:
  0.0 765.6 jit_solution(790524360846847790)
XLA Ops:
  3.2 144.3 %all-gather = f32[1,1,3072,16]{3,1,0,2:T(1,128)S(1)} all-gather(f32[1,1,6,16]{3,1,0,2:T(1,128)} %bitcast.283), channel_id=2, replica_groups=mesh['sub'=64,'grp'=8] {'sub','grp'}, dimensions={2}, use_global_device_ids=true | all-gather | bytes 196992 | tf_op jit(solution)/shard_map/all_gather | solution.py:79
  150.8 8.4 %gather_fusion.1 = f32[1536]{0:T(1024)S(1)} fusion(f32[1536]{0:T(1024)S(1)} %reduce.3, s32[2048]{0:T(1024)S(1)} %pad_clamp_fusion.2), kind=kCustom, calls=%fused_computation.4 | custom fusion | bytes 18432 | tf_op jit(solution)/shard_map/jit(_take)/gather | solution.py:61
  166.4 5.0 sort.17
  171.5 13.3 %gather_fusion.2 = bf16[1536,1536]{1,0:T(8,128)(2,1)} fusion(bf16[1536,1536]{1,0:T(8,128)(2,1)} %bitcast.245, s32[2048]{0:T(1024)S(1)} %pad_clamp_fusion.2), kind=kCustom, calls=%fused_computation.5 | custom fusion | bytes 9443328 | tf_op jit(solution)/shard_map/jit(_take)/gather | solution.py:58
  184.8 5.0 broadcast_select_fusion
  189.8 6.7 copy.183
  196.4 13.4 %gather_fusion.3 = bf16[1536,1536]{1,0:T(8,128)(2,1)} fusion(bf16[1536,1536]{0,1:T(8,128)(2,1)} %copy.183, s32[2048]{0:T(1024)S(1)} %pad_clamp_fusion.2), kind=kCustom, calls=%fused_computation.6 | custom fusion | bytes 9443328 | tf_op jit(solution)/shard_map/jit(_take)/gather | solution.py:58
  217.3 3.3 collective-permute-done.2
  220.6 4.1 collective-permute-done.3
  225.0 3.6 convolution_subtract_fusion
  240.2 4.0 collective-permute-done.7
  246.1 108.5 %all-gather.1 = f32[512,6,16]{2,1,0:T(8,128)S(1)} all-gather(f32[1,6,16]{2,1,0:T(8,128)S(1)} %convolution_bitcast_fusion.2), channel_id=1, replica_groups=mesh['sub'=64,'grp'=8] {'sub','grp'}, dimensions={0}, use_global_device_ids=true | all-gather | bytes 196992 | tf_op jit(solution)/shard_map/all_gather | solution.py:79
  364.5 3.1 collective-permute-done.9
  372.4 4.0 collective-permute-done.11
  378.4 106.9 %all-gather.2 = f32[512,6,16]{2,1,0:T(8,128)S(1)} all-gather(f32[1,6,16]{2,1,0:T(8,128)S(1)} %convolution_bitcast_fusion.1), channel_id=1, replica_groups=mesh['sub'=64,'grp'=8] {'sub','grp'}, dimensions={0}, use_global_device_ids=true | all-gather | bytes 196992 | tf_op jit(solution)/shard_map/all_gather | solution.py:79
  498.4 3.4 collective-permute-start.14
  503.7 4.0 collective-permute-done.15
  508.0 3.6 fusion
  516.8 3.6 collective-permute-done.17
  525.5 3.8 collective-permute-done.19
  529.7 102.0 %all-reduce = (f32[16]{0:T(128)S(1)}, f32[16]{0:T(128)S(1)}) all-reduce(f32[16]{0:T(128)S(1)} %get-tuple-element.22, f32[16]{0:T(128)S(1)} %get-tuple-element.20), channel_id=1, replica_groups=mesh['sub'=64,'grp'=8] {'sub','grp'}, use_global_device_ids=true, to_apply=%region_1.3 | all-reduce | flops 32 | bytes 256 | tf_op jit(solution)/shard_map/psum | solution.py:115
  633.4 101.9 %all-gather.3 = f32[512,6,16]{2,1,0:T(8,128)S(1)} all-gather(f32[1,6,16]{2,1,0:T(8,128)S(1)} %convolution_bitcast_fusion), channel_id=1, replica_groups=mesh['sub'=64,'grp'=8] {'sub','grp'}, dimensions={0}, use_global_device_ids=true | all-gather | bytes 196992 | tf_op jit(solution)/shard_map/all_gather | solution.py:79
  748.3 3.3 collective-permute-start.22
  753.5 4.0 collective-permute-done.23
  (225 shorter events, 100.6 us)
Async XLA Ops:
  161.9 51.2 %collective-permute-start = (f32[1,2,17,512]{3,2,1,0:T(8,128)S(1)}, f32[1,2,17,512]{3,2,1,0:T(8,128)S(1)}, u32[]{:S(2)}, u32[]{:S(2)}) collective-permute-start(f32[1,2,17,512]{3,2,1,0:T(8,128)S(1)} %maximum_bitcast_fusion), channel_id=1, source_target_pairs={{0,8},{8,16},{16,24},{24,32},{32,40},{40,48},{48,56},{56,64},{64,7... | collective-permute-start | bytes 208904 | tf_op jit(solution)/shard_map/ppermute | solution.py:14
  164.0 49.2 %collective-permute-start.1 = (f32[1,2,17,512]{3,2,1,0:T(8,128)S(1)}, f32[1,2,17,512]{3,2,1,0:T(8,128)S(1)}, u32[]{:S(2)}, u32[]{:S(2)}) collective-permute-start(f32[1,2,17,512]{3,2,1,0:T(8,128)S(1)} %copy.175), channel_id=1, source_target_pairs={{8,0},{16,8},{24,16},{32,24},{40,32},{48,40},{56,48},{64,56},{72,6... | collective-permute-start | bytes 208904 | tf_op jit(solution)/shard_map/ppermute | solution.py:15
  213.3 7.3 collective-permute-start.2
  216.0 8.7 %collective-permute-start.3 = (f32[4,1,17,512]{3,2,1,0:T(8,128)S(1)}, f32[4,1,17,512]{3,2,1,0:T(8,128)S(1)}, u32[]{:S(2)}, u32[]{:S(2)}) collective-permute-start(f32[4,1,17,512]{3,2,1,0:T(8,128)S(1)} %get-tuple-element.26), channel_id=1, source_target_pairs={{1,0},{2,1},{3,2},{4,3},{5,4},{6,5},{7,6},{9,8},{10,9},{11,10},{12... | collective-permute-start | bytes 417800 | tf_op jit(solution)/shard_map/ppermute | solution.py:15
  228.8 4.6 collective-permute-start.4
  230.9 5.6 collective-permute-start.5
  236.5 3.7 collective-permute-start.6
  238.3 5.9 collective-permute-start.7
  360.1 4.4 collective-permute-start.8
  362.0 5.6 collective-permute-start.9
  367.6 4.8 collective-permute-start.10
  370.5 5.9 collective-permute-start.11
  490.8 4.4 collective-permute-start.12
  492.7 5.6 collective-permute-start.13
  498.4 5.3 collective-permute-start.14
  501.8 5.9 collective-permute-start.15
  511.7 5.0 collective-permute-start.16
  514.9 5.6 collective-permute-start.17
  520.5 5.0 collective-permute-start.18
  523.6 5.8 collective-permute-start.19
  740.8 4.9 collective-permute-start.20
  742.7 5.6 collective-permute-start.21
  748.3 5.2 collective-permute-start.22
  751.6 5.9 collective-permute-start.23
  (2 other events, 172.0 us)
where the time goes:
time: 768 us; the launch traced here: 766 us
  blocking collectives  564 us (73%)
  local copies, waits for them, and re-layouts  63.2 us (8%)
  starting transfers between devices  51.9 us (7%)
  waiting for transfers between devices  45.4 us (6%)
  matrix products  26.3 us (3%)
  other arithmetic  13.3 us (2%)
    all_gather x4, blocking collectives, coarse(): gathered = lax.all_gather(local_sums, ('sub', 'grp'), axis=0, tiled=True)  462 us
    psum x1, blocking collectives, body(): lax.psum(jnp.sum(weights * scaling * projected * projected, axis=1), ('su...  102 us
    ppermute x12, waiting for transfers between devices, extended_2(): after = lax.ppermute(initial, axis, down)  39.4 us
    ppermute x12, starting transfers between devices, extended_2(): before = lax.ppermute(last, axis, up)  29.9 us
    ppermute x12, starting transfers between devices, extended_2(): after = lax.ppermute(initial, axis, down)  21.9 us
  transfers between devices with their start and end apart: 24, of which 17 were waited for; matrix products, arithmetic and copies ran while one was open for 6% of the time, Pallas kernels for 0%

commit v1 on v0

v1 whole, which is shorter than its diff:
```python
import functools

import jax
import jax.numpy as jnp
from jax import lax
from jax.experimental import pallas as pl
from jax.experimental.pallas import tpu as pltpu
from jax.sharding import PartitionSpec as P

MESH = pl.DeviceIdType.MESH
F32 = jnp.float32
BF16 = jnp.bfloat16

INTF = 1536
FACE = 256
NC = 3072
NRHS = 16
MODES = 6
ROWS = 48


def dot(a, b):
    return lax.dot_general(a, b, (((1,), (0,)), ((), ())), preferred_element_type=F32)


def dot_nt(a, b):
    return lax.dot_general(a, b, (((1,), (1,)), ((), ())), preferred_element_type=F32)


def split(x):
    high = x.astype(BF16)
    return high, (x - high.astype(F32)).astype(BF16)


def split3(x):
    high = x.astype(BF16)
    rest = x - high.astype(F32)
    middle = rest.astype(BF16)
    return high, middle, (rest - middle.astype(F32)).astype(BF16)


def hops(k, n):
    return min(k, n - k)


def wrap(v, n):
    return jnp.where(v >= n, v - n, v)


def kernel(
    schur_hbm, load_ref, modes_ref, stiff_ref, coarse_ref, rigid_ref, order_ref,
    mult_ref, proj_ref, amp_ref,
    schur, onehot, permuted, small, small_slot, coarse_raw, coarse_hot, coarse_mat,
    lift_slot_mat, lift_dof_mat, modes_ext, face_static, gathered, sent, received, scaling,
    row_ref,
    schur_sem, g_send, g_recv, c_send, c_recv, f_send, f_recv, x_send, x_recv,
):
    sub = lax.axis_index("sub")
    b = lax.axis_index("grp")
    x = lax.div(sub, 16)
    y = lax.rem(lax.div(sub, 2), 8)
    core = lax.rem(sub, 2)
    tile = (x * 2 + core) * 8 + y

    def at(dx, dy, dz):
        return {"sub": (wrap(x + dx, 4) * 8 + wrap(y + dy, 8)) * 2 + core, "grp": wrap(b + dz, 8)}

    along_z = sorted([(0, 0, k) for k in range(1, 8)], key=lambda t: -hops(t[2], 8))
    along_xy = sorted(
        [(i, j, 0) for i in range(4) for j in range(8) if i or j],
        key=lambda t: -(hops(t[0], 4) + hops(t[1], 8)),
    )
    other_core = {"sub": sub + 1 - 2 * core, "grp": b}
    beside = [
        {"sub": wrap(sub + 63, 64), "grp": b},
        {"sub": wrap(sub + 1, 64), "grp": b},
        {"sub": sub, "grp": wrap(b + 7, 8)},
        {"sub": sub, "grp": wrap(b + 1, 8)},
    ]
    exists = [sub > 0, sub < 63, b > 0, b < 7]

    barrier = pltpu.get_barrier_semaphore()
    partners = [at(*t) for t in along_xy + along_z] + beside[:2]
    for partner in partners:
        pl.semaphore_signal(barrier, inc=1, device_id=partner, device_id_type=MESH)
    schur_copy = pltpu.make_async_copy(schur_hbm.at[0, 0], schur, schur_sem)
    schur_copy.start()

    def remote(src, dst, send, recv, device):
        pltpu.make_async_remote_copy(
            src_ref=src, dst_ref=dst, send_sem=send, recv_sem=recv,
            device_id=device, device_id_type=MESH,
        ).start()

    def wait(ref, sem):
        pltpu.make_async_copy(ref, ref, sem).wait()

    def own_row(g):
        return gathered.at[g, tile, pl.ds(b, 1)]

    def start_z(g, row):
        gathered[g, tile, pl.ds(b, 1)] = row
        for t in along_z:
            remote(own_row(g), own_row(g), g_send.at[g, 0], g_recv.at[g, 0], at(*t))

    def wait_z(g):
        wait(gathered.at[g, 0, pl.ds(0, 7)], g_recv.at[g, 0])

    def start_xy(g):
        column = gathered.at[g, tile]
        for t in along_xy:
            remote(column, column, g_send.at[g, 1], g_recv.at[g, 1], at(*t))

    def wait_xy(g):
        wait(gathered.at[g, pl.ds(0, 31)], g_recv.at[g, 1])

    def start_core(g):
        for i in range(4):
            part = gathered.at[g, pl.ds((2 * i + core) * 8, 8)]
            remote(part, part, g_send.at[g, 2], g_recv.at[g, 2], other_core)

    def wait_core(g):
        wait(gathered.at[g, pl.ds(0, 32)], g_recv.at[g, 2])

    def exchange(g):
        for f in range(4):
            remote(
                sent.at[g, :, pl.ds(f * FACE, FACE)], received.at[g, f ^ 1],
                x_send.at[g, f], x_recv.at[g, f ^ 1], beside[f],
            )
        for f in range(4):
            wait(received.at[g, f], x_recv.at[g, f])

    order = order_ref[...].reshape(1, INTF)

    def make_onehot(i, carry):
        rows = pl.ds(pl.multiple_of(i * 128, 128), 128)
        dofs = lax.broadcasted_iota(jnp.int32, (128, INTF), 0) + i * 128
        onehot[rows, :] = jnp.where(dofs == order, 1.0, 0.0).astype(BF16)
        return carry

    lax.fori_loop(0, INTF // 128, make_onehot, 0)
    small[...] = jnp.zeros_like(small)
    small[0:MODES, :] = modes_ref[0, 0]
    small[MODES : MODES + 1, :] = stiff_ref[0]
    small[8:24, :] = load_ref[0, 0]
    pieces = split3(jnp.concatenate([small[...], jnp.zeros((8, INTF), F32)], axis=0))
    stacked = dot(jnp.concatenate(pieces, axis=0), onehot[...])
    small_slot[...] = (stacked[0:32] + stacked[32:64] + stacked[64:96])[0:24]
    face_static[0] = small_slot[0:8, 0 : 4 * FACE]
    coarse_raw[0] = jnp.zeros((8, NC), F32)
    coarse_raw[5] = jnp.zeros((8, NC), F32)
    coarse_raw[0, 0:MODES] = coarse_ref[...]
    lanes = lax.broadcasted_iota(jnp.int32, (8, 128), 1)
    row_ref[...] = jnp.zeros_like(row_ref)
    row_ref[0:MODES, 0:NRHS] = rigid_ref[0, 0]
    rigid = row_ref[...]
    row = rigid[0:1]
    for m in range(1, MODES):
        row = row + pltpu.roll(rigid[m : m + 1], NRHS * m, 1)

    pl.semaphore_wait(barrier, len(partners))

    start_z(0, row)
    for f in range(4):
        remote(
            face_static.at[0, :, pl.ds(f * FACE, FACE)], face_static.at[1, :, pl.ds((f ^ 1) * FACE, FACE)],
            f_send.at[f], f_recv.at[f ^ 1], beside[f],
        )
    for f in range(4):
        remote(
            coarse_raw.at[0], coarse_raw.at[1 + (f ^ 1)],
            c_send.at[f], c_recv.at[f ^ 1], beside[f],
        )
    schur_copy.wait()

    def permute(i, carry):
        columns = pl.ds(pl.multiple_of(i * FACE, FACE), FACE)

        def part(j, inner):
            rows = pl.ds(pl.multiple_of(j * 512, 512), 512)
            permuted[rows, columns] = dot(schur[rows, :], onehot[:, columns]).astype(BF16)
            return inner

        return lax.fori_loop(0, 3, part, carry)

    lax.fori_loop(0, 2, permute, 0)
    wait_z(0)
    start_xy(0)

    for f in range(4):
        wait(face_static.at[1, :, pl.ds(f * FACE, FACE)], f_recv.at[f])
    modes_ext[...] = jnp.zeros_like(modes_ext)
    modes_ext[0:MODES, :] = small_slot[0:MODES, :]
    scaling[...] = small_slot[MODES : MODES + 1, :]
    for f in range(4):
        columns = slice(f * FACE, (f + 1) * FACE)
        arrived = jnp.where(exists[f], face_static[1, :, columns], 0.0)
        modes_ext[8 + 8 * f : 8 + 8 * f + MODES, columns] = -arrived[0:MODES]
        scaling[:, columns] = scaling[:, columns] + arrived[MODES : MODES + 1]
    ext_high, ext_low = split(modes_ext[...])
    lift_slot_mat[:, 0:INTF] = ext_high
    lift_slot_mat[:, INTF : 2 * INTF] = ext_low
    lift_dof_mat[:, 0:INTF] = dot_nt(ext_high, onehot[...]).astype(BF16)
    lift_dof_mat[:, INTF : 2 * INTF] = dot_nt(ext_low, onehot[...]).astype(BF16)

    out_pos = lax.broadcasted_iota(jnp.int32, (1, 768), 1)
    place = out_pos % 128
    source = (((place // 8) % 8 * 2 + place // 64) * 8 + place % 8) * MODES + out_pos // 128
    coarse_hot[...] = jnp.where(
        lax.broadcasted_iota(jnp.int32, (768, 768), 0) == source, 1.0, 0.0
    ).astype(BF16)
    for f in range(4):
        wait(coarse_raw.at[1 + f], c_recv.at[f])
    for k in range(4):
        chunk = coarse_raw[:, :, 768 * k : 768 * (k + 1)].reshape(ROWS, 768)
        sorted_rows = dot(jnp.concatenate(split(chunk), axis=0), coarse_hot[...]).astype(BF16)
        for part in range(2):
            for m in range(MODES):
                coarse_mat[
                    (part * MODES + m) * ROWS : (part * MODES + m + 1) * ROWS, 128 * k : 128 * (k + 1)
                ] = sorted_rows[part * ROWS : (part + 1) * ROWS, 128 * m : 128 * (m + 1)]

    lax.fori_loop(2, 4, permute, 0)
    wait_xy(0)
    start_core(0)
    lax.fori_loop(4, 6, permute, 0)
    wait_core(0)

    own_modes = small_slot[0:8, :]
    load = small_slot[8:24, :]
    groups = lax.broadcasted_iota(jnp.int32, (ROWS, 128), 1) // NRHS

    def coarse(g):
        everyone = gathered[g].reshape(512, 128)
        high, low = split(everyone)
        product = dot(coarse_mat[...], jnp.concatenate([high, low], axis=1))
        half = MODES * ROWS
        z = product[0:half, 0:128] + product[0:half, 128:256] + product[half:, 0:128]
        picked = jnp.zeros((ROWS, 128), F32)
        for m in range(MODES):
            picked = jnp.where(groups == m, z[m * ROWS : (m + 1) * ROWS], picked)
        total = jnp.sum(everyone, axis=0, keepdims=True)
        last = lax.broadcasted_iota(jnp.int32, (ROWS, 128), 0) == ROWS - 1
        picked = jnp.where(last, total, picked)
        turned = jnp.transpose(jnp.concatenate([picked, jnp.zeros((128 - ROWS, 128), F32)], axis=0))
        amplitudes = turned[0:NRHS]
        for m in range(1, MODES):
            amplitudes = amplitudes + turned[m * NRHS : (m + 1) * NRHS]
        return amplitudes[:, 0:ROWS], turned[6 * NRHS : 7 * NRHS, ROWS - 1 : ROWS]

    def lift(amplitudes, matrix):
        product = dot(jnp.concatenate(split(amplitudes), axis=0), matrix[...])
        return product[0:NRHS, 0:INTF] + product[0:NRHS, INTF:] + product[NRHS:, 0:INTF]

    case = lax.broadcasted_iota(jnp.int32, (NRHS, 128), 0)
    lane = lax.broadcasted_iota(jnp.int32, (NRHS, 128), 1)

    def rows_of(values, extra=None):
        spread = jnp.zeros((NRHS, 128), F32)
        for m in range(MODES):
            column = jnp.sum(values * own_modes[m : m + 1], axis=1, keepdims=True)
            spread = jnp.where(lane == m * NRHS + case, column, spread)
        if extra is not None:
            spread = jnp.where(lane == MODES * NRHS + case, extra, spread)
        return jnp.sum(spread, axis=0, keepdims=True)

    def to_dof(values):
        product = dot_nt(jnp.concatenate(split3(values), axis=0), onehot[...])
        return product[0:NRHS] + product[NRHS : 2 * NRHS] + product[2 * NRHS :]

    def subtract_beside(g, values):
        parts = [
            values[:, f * FACE : (f + 1) * FACE] - jnp.where(exists[f], received[g, f], 0.0)
            for f in range(4)
        ]
        return jnp.concatenate(parts + [values[:, 4 * FACE :]], axis=1)

    multipliers, unused = coarse(0)
    multipliers = lift(multipliers, lift_dof_mat)
    sent[0] = load - dot(multipliers.astype(BF16), permuted[...])
    exchange(0)
    residual = subtract_beside(0, sent[0])

    start_z(1, rows_of(residual))
    residual_dof = to_dof(residual)
    wait_z(1)
    start_xy(1)
    wait_xy(1)
    start_core(1)
    wait_core(1)
    amplitudes, unused = coarse(1)
    projected = residual - lift(amplitudes, lift_slot_mat)
    scaled = scaling[...] * projected
    weights = jnp.concatenate(
        [jnp.full((1, FACE), jnp.where(e, 0.5, 1.0), F32) for e in exists] + [jnp.full((1, 2 * FACE), 1.0, F32)],
        axis=1,
    )
    norm_part = jnp.sum(weights * projected * scaled, axis=1, keepdims=True)

    start_z(2, rows_of(scaled, norm_part))
    scaled_dof = to_dof(scaled)
    wait_z(2)
    start_xy(2)
    wait_xy(2)
    start_core(2)
    wait_core(2)
    direction_amplitudes, norm = coarse(2)
    direction_dof = scaled_dof - lift(direction_amplitudes, lift_dof_mat)
    image_local = dot(direction_dof.astype(BF16), permuted[...])
    sent[1] = image_local
    direction = scaled - lift(direction_amplitudes, lift_slot_mat)
    curvature_part = jnp.sum(direction * image_local, axis=1, keepdims=True)
    exchange(1)
    image = subtract_beside(1, sent[1])

    start_z(3, rows_of(image, curvature_part))
    image_dof = to_dof(image)
    wait_z(3)
    start_xy(3)
    wait_xy(3)
    start_core(3)
    wait_core(3)
    image_amplitudes, curvature = coarse(3)
    step = norm / curvature
    mult_ref[0, 0] = multipliers + step * direction_dof
    amplitudes = amplitudes - step * image_amplitudes
    proj_ref[0, 0] = residual_dof - step * image_dof - lift(amplitudes, lift_dof_mat)
    amp_ref[0, 0] = jnp.transpose(
        jnp.concatenate([amplitudes, jnp.zeros((NRHS, 128 - ROWS), F32)], axis=1)
    )[0:MODES, :]

    for g in range(4):
        wait(gathered.at[g, 0, pl.ds(0, 7)], g_send.at[g, 0])
        wait(gathered.at[g, pl.ds(0, 31)], g_send.at[g, 1])
        wait(gathered.at[g, pl.ds(0, 32)], g_send.at[g, 2])
    for f in range(4):
        wait(face_static.at[1, :, pl.ds(f * FACE, FACE)], f_send.at[f])
        wait(coarse_raw.at[1 + f], c_send.at[f])
        for g in range(2):
            wait(received.at[g, f], x_send.at[g, f])


def body(schur, dual_load, modes, diag_stiff, coarse_inverse, rigid_loads, face_index):
    vmem = pl.BlockSpec(memory_space=pltpu.VMEM)
    return pl.pallas_call(
        kernel,
        out_shape=(
            jax.ShapeDtypeStruct((1, 1, NRHS, INTF), F32),
            jax.ShapeDtypeStruct((1, 1, NRHS, INTF), F32),
            jax.ShapeDtypeStruct((1, 1, MODES, NRHS), F32),
        ),
        in_specs=[pl.BlockSpec(memory_space=pl.ANY)] + [vmem] * 6,
        out_specs=(vmem, vmem, vmem),
        scratch_shapes=[
            pltpu.VMEM((INTF, INTF), BF16),
            pltpu.VMEM((INTF, INTF), BF16),
            pltpu.VMEM((INTF, INTF), BF16),
            pltpu.VMEM((24, INTF), F32),
            pltpu.VMEM((24, INTF), F32),
            pltpu.VMEM((6, 8, NC), F32),
            pltpu.VMEM((768, 768), BF16),
            pltpu.VMEM((2 * MODES * ROWS, 512), BF16),
            pltpu.VMEM((ROWS, 2 * INTF), BF16),
            pltpu.VMEM((ROWS, 2 * INTF), BF16),
            pltpu.VMEM((ROWS, INTF), F32),
            pltpu.VMEM((2, 8, 4 * FACE), F32),
            pltpu.VMEM((4, 64, 8, 128), F32),
            pltpu.VMEM((2, NRHS, INTF), F32),
            pltpu.VMEM((2, 4, NRHS, FACE), F32),
            pltpu.VMEM((1, INTF), F32),
            pltpu.VMEM((8, 128), F32),
            pltpu.SemaphoreType.DMA,
            pltpu.SemaphoreType.DMA((4, 3)),
            pltpu.SemaphoreType.DMA((4, 3)),
            pltpu.SemaphoreType.DMA((4,)),
            pltpu.SemaphoreType.DMA((4,)),
            pltpu.SemaphoreType.DMA((4,)),
            pltpu.SemaphoreType.DMA((4,)),
            pltpu.SemaphoreType.DMA((2, 4)),
            pltpu.SemaphoreType.DMA((2, 4)),
        ],
        compiler_params=pltpu.CompilerParams(
            collective_id=0, has_side_effects=True, vmem_limit_bytes=48 * 2**20
        ),
    )(schur, dual_load, modes, diag_stiff, coarse_inverse, rigid_loads, face_index)


def solution(mesh):
    placed = (
        P("sub", "grp", None, None),
        P("sub", "grp", None, None),
        P("sub", "grp", None, None),
        P("sub", "grp", None),
        P(("sub", "grp"), None),
        P("sub", "grp", None, None),
        P("sub", "grp", None),
    )
    return jax.shard_map(
        body,
        mesh=mesh,
        in_specs=placed,
        out_specs=(
            P("sub", "grp", None, None),
            P("sub", "grp", None, None),
            P("sub", "grp", None, None),
        ),
        check_vma=False,
    )
```

time: 768 us -> 88.8 us (0.12)
  blocking collectives: 564 us -> 0 us
  Pallas kernels: 0 us -> 79 us
  local copies, waits for them, and re-layouts: 63.2 us -> 8.82 us
  starting transfers between devices: 51.9 us -> 0 us
  waiting for transfers between devices: 45.4 us -> 0 us
  matrix products: 26.3 us -> 0 us
  other arithmetic: 13.3 us -> 0 us
    all_gather x4 -> x0, blocking collectives: 462 us -> none  [coarse(): gathered = lax.all_gather(local_sums, ('sub', 'grp'), axis=0, tiled=True)]
    psum x1 -> x0, blocking collectives: 102 us -> none  [body(): lax.psum(jnp.sum(weights * scaling * projected * projected, axis=1), ('su...]
    pallas_call x0 -> x1, Pallas kernels: none -> 79 us  [body(): pl.pallas_call(kernel, out_shape=(jax.ShapeDtypeStruct((1, 1, NRHS, INTF)...]
    ppermute x24 -> x0, starting transfers between devices: 51.9 us -> none  [the longest x12 29.9 us: extended_2(): before = lax.ppermute(last, axis, up)]
    gather x9 -> x0, local copies, waits for them, and re-layouts: 45.7 us -> none  [the longest x1 13.4 us: body(): jnp.take(jnp.take(schur[0, 0], ordering, axis=0), ordering, axis=1)]
    ppermute x24 -> x0, waiting for transfers between devices: 45.4 us -> none  [the longest x12 39.4 us: extended_2(): after = lax.ppermute(initial, axis, down)]
    dot_general x13 -> x0, matrix products: 26.3 us -> none  [the longest x4 7.81 us: coarse(): jnp.dot(coarse_inverse, gathered, precision=lax.Precision.HIGHEST, prefer...]
  transfers between devices with their start and end apart: 24 -> 0, of which waited for: 17 -> 0; matrix products, arithmetic and copies ran while one was open for 6% -> 0% of each run, Pallas kernels for 0% -> 0%
where the time goes in v1:
time: 88.8 us; the launch traced here: 88.4 us
  Pallas kernels  79 us (89%)
  local copies, waits for them, and re-layouts  8.82 us (10%)
    pallas_call x1, Pallas kernels, body(): pl.pallas_call(kernel, out_shape=(jax.ShapeDtypeStruct((1, 1, NRHS, INTF)...  79 us
    unnamed x14, local copies, waits for them, and re-layouts  8.24 us

profile of v1, /device:TPU:1, one launch (start us, length us, event | category | flops | bytes accessed | tf_op | source)
XLA Modules:
  0.0 88.4 jit_solution(5264175348347885416)
XLA Ops:
  0.6 0.7 copy.11.rigid_ref
  1.3 0.8 copy.10.modes_ref
  2.1 0.0 copy-start
  2.1 2.3 %copy-done = bf16[1,1,1536,1536]{3,2,1,0:T(8,128)(2,1)S(1)} copy-done((bf16[1,1,1536,1536]{3,2,1,0:T(8,128)(2,1)S(1)}, bf16[1,1,1536,1536]{3,2,1,0:T(8,128)(2,1)}, u32[]{:S(2)}) %copy-start) | copy-done | bytes 4718616
  4.4 0.0 copy-start.1
  4.4 0.9 %copy-done.1 = f32[1,1,16,1536]{3,2,1,0:T(8,128)S(1)} copy-done((f32[1,1,16,1536]{3,2,1,0:T(8,128)S(1)}, f32[1,1,16,1536]{3,2,1,0:T(8,128)}, u32[]{:S(2)}) %copy-start.1) | copy-done | bytes 98328
  5.3 0.0 copy-start.2
  5.3 0.9 %copy-done.2 = f32[6,3072]{1,0:T(8,128)S(1)} copy-done((f32[6,3072]{1,0:T(8,128)S(1)}, f32[6,3072]{1,0:T(8,128)}, u32[]{:S(2)}) %copy-start.2) | copy-done | bytes 73752
  6.2 0.0 copy-start.3
  6.2 0.7 copy-done.3
  6.9 0.0 copy-start.4
  6.9 0.7 copy-done.4
  7.6 79.0 %shard_map.94 = (f32[1,1,16,1536]{3,2,1,0:T(8,128)S(1)}, f32[1,1,16,1536]{3,2,1,0:T(8,128)S(1)}, f32[1,1,6,16]{3,2,1,0:T(8,128)S(1)}) custom-call(bf16[1,1,1536,1536]{3,2,1,0:T(8,128)(2,1)S(1)} %copy-done, f32[1,1,16,1536]{3,2,1,0:T(8,128)S(1)} %copy-done.1, f32[1,1,6,1536]{3,2,1,0:T(8,128)S(1)} %copy.10.modes_ref, f32[1,1,1536]{2,1,0:T(1,128)S(1)} %copy-done.3, ...), custom_call_target="tpu_custom_call" | custom-call | tf_op jit(solution)/shard_map/pallas_call | solution.py:346
  86.6 0.6 copy.12
  87.2 0.6 copy.15
  87.8 0.6 copy.16
Async XLA Ops:
  2.1 2.3 %copy-start = (bf16[1,1,1536,1536]{3,2,1,0:T(8,128)(2,1)S(1)}, bf16[1,1,1536,1536]{3,2,1,0:T(8,128)(2,1)}, u32[]{:S(2)}) copy-start(bf16[1,1,1536,1536]{3,2,1,0:T(8,128)(2,1)} %schur_hbm.1) | copy-start | bytes 14155780
  4.4 0.9 %copy-start.1 = (f32[1,1,16,1536]{3,2,1,0:T(8,128)S(1)}, f32[1,1,16,1536]{3,2,1,0:T(8,128)}, u32[]{:S(2)}) copy-start(f32[1,1,16,1536]{3,2,1,0:T(8,128)} %load_ref.1) | copy-start | bytes 294916
  5.3 0.9 %copy-start.2 = (f32[6,3072]{1,0:T(8,128)S(1)}, f32[6,3072]{1,0:T(8,128)}, u32[]{:S(2)}) copy-start(f32[6,3072]{1,0:T(8,128)} %coarse_ref.1) | copy-start | bytes 221188
  6.2 0.7 copy-start.3
  6.9 0.7 copy-start.4
